TPU v7x, 32 devices: a whole 2x2x4 slice. The times are simulated.
32 devices in a mesh: seq: 8 (over z, y), nb: 4 (over x, core).
Axes of the slice: x: 2, y: 2, z: 4, core: 2. Of those that a mesh axis runs over, the one named last changes fastest.
Arguments:
- q_self: bfloat16 [2048, 4096], P('seq', 'nb'), may hold values from -6 to 6
- k_self: bfloat16 [2048, 4096], P('seq', 'nb'), may hold values from -6 to 6
- v_self: bfloat16 [2048, 4096], P('seq', 'nb'), may hold values from -6 to 6
- q_cca: bfloat16 [2048, 4096], P('seq', 'nb'), may hold values from -6 to 6
- memory: bfloat16 [2048, 2, 1024], P('seq'), may hold values from -6 to 6
- database: bfloat16 [8192, 2048], P(('seq', 'nb')), may hold values from -6 to 6
- nbr_block: int32 [512], P(('seq', 'nb')), may hold values from 0 to 63, as said below
- span_offset: int32 [32], P('seq'), may hold values from 1 to 63
- enc_query: bfloat16 [2048, 1024], P('seq'), may hold values from -0.1355122 to 0.1355122
- enc_out: bfloat16 [1024, 2048], P('seq'), may hold values from -0.1875 to 0.1875
- enc_gain: float32 [2048], replicated, may hold values from 0.5 to 1.5
- cca_kv: bfloat16 [2048, 2, 4096], P(None, None, 'nb'), may hold values from -0.134535646 to 0.134535646
Outputs:
- attended: bfloat16 [2048, 4096], P('seq', 'nb')
Inputs may be any that keep to these rules, and one draw needn't show every extreme that they name: `nbr_block`: block ids are local to a group of 4 devices along nb; the owner of id g is nb index g // 16. Among the 16 requests of one device at most 12 name blocks of one owner, and exactly 12 name blocks of some owner.
All inputs are finite; a program needn't handle non-finite values.
Results may differ from a plain program's by a relative error of at most 0.0041.
Values may be sent and summed in bfloat16 or wider, within the bound.
A program may use at most 192 MiB of HBM per device.

v0:
```python
import jax
import jax.numpy as jnp
from jax import lax
from jax.sharding import PartitionSpec as P

HD = 128
E = 2048
SPAN = 64
K = 2
R = 128
BLK = 16


masked_score = -1e30


def passed_along(block, axis, distance):
    devices = range(lax.axis_size(axis))
    route = [(i - distance, i) for i in devices if i - distance in devices]
    return lax.ppermute(block, axis, route)


def local(
    q_self,
    k_self,
    v_self,
    q_cca,
    memory,
    database,
    nbr_block,
    span_offset,
    enc_query,
    enc_out,
    enc_gain,
    cca_kv,
):
    tokens_here = q_self.shape[0]
    head_cols = q_self.shape[1]
    head_count = head_cols // HD
    score_scale = HD ** (-0.5)
    query_start = lax.axis_index("seq") * tokens_here
    query_pos = query_start + jnp.arange(tokens_here, dtype=jnp.int32)
    queries = q_self.reshape(tokens_here, head_count, HD)
    key_part = lax.all_gather(k_self, "seq", axis=0, tiled=True)
    value_part = lax.all_gather(v_self, "seq", axis=0, tiled=True)
    key_count = key_part.shape[0]
    scores = (
        jnp.einsum(
            "qhd,khd->hqk",
            queries,
            key_part.reshape(key_count, head_count, HD),
            preferred_element_type=jnp.float32,
        )
        * score_scale
    )
    key_pos = jnp.arange(key_count, dtype=jnp.int32)
    allowed = (key_pos[None, :] <= query_pos[:, None])[None]
    scores = jnp.where(allowed, scores, masked_score)
    old_max = jnp.full((head_count, tokens_here), masked_score, jnp.float32)
    new_max = jnp.maximum(old_max, jnp.max(scores, axis=2))
    weights_raw = jnp.where(allowed, jnp.exp(scores - new_max[:, :, None]), 0.0)
    new_sum = jnp.sum(weights_raw, axis=2)
    added = jnp.einsum(
        "hqk,khd->hqd",
        weights_raw.astype(jnp.bfloat16),
        value_part.reshape(key_count, head_count, HD),
        preferred_element_type=jnp.float32,
    )
    self_out = (added / new_sum[:, :, None]).transpose(1, 0, 2).reshape(tokens_here, head_cols)
    query_full, output_full = (
        lax.all_gather(enc_query, "seq", axis=0, tiled=True),
        lax.all_gather(enc_out, "seq", axis=0, tiled=True),
    )
    enc_heads = memory.shape[2] // HD
    memory_keys = memory[:, 0].reshape(tokens_here, enc_heads, HD)
    memory_values = memory[:, 1].reshape(tokens_here, enc_heads, HD)
    key_span = jnp.arange(tokens_here, dtype=jnp.int32) // SPAN
    key_open = jnp.arange(tokens_here, dtype=jnp.int32) % SPAN < jnp.repeat(span_offset, SPAN)
    request_count = nbr_block.shape[0]
    owners = lax.axis_size("nb")
    db_count = database.shape[0] // BLK
    capacity = max(2, 3 * request_count // owners)
    owner_ids = nbr_block // db_count
    local_block = nbr_block % db_count
    owner_hits = (owner_ids[:, None] == jnp.arange(owners, dtype=jnp.int32)[None, :]).astype(
        jnp.int32
    )
    rank_within = jnp.sum((jnp.cumsum(owner_hits, axis=0) - 1) * owner_hits, axis=1)
    slot_index = owner_ids * capacity + rank_within
    blocks_span = K * (R // BLK)
    request_place = (
        lax.axis_index("nb") * request_count + jnp.arange(request_count, dtype=jnp.int32) + 1
    )
    request_span = (request_place - 1) // blocks_span
    slot_match = slot_index[None, :] == jnp.arange(owners * capacity, dtype=jnp.int32)[:, None]
    sent_block = jnp.sum(jnp.where(slot_match, local_block[None, :], 0), axis=1)
    sent_span = jnp.sum(jnp.where(slot_match, request_span[None, :], 0), axis=1)
    sent_place = jnp.sum(jnp.where(slot_match, request_place[None, :], 0), axis=1)
    packed = jnp.stack([sent_block, sent_span, sent_place], axis=-1).reshape(owners, capacity, 3)
    db_blocks = database.reshape(db_count, BLK, E)
    request_rows = lax.all_to_all(packed, "nb", split_axis=0, concat_axis=0, tiled=True)
    slot_count = request_rows.shape[1]
    fetched = db_blocks[request_rows[:, :, 0].reshape(-1)].reshape(-1, E)
    span_rows = jnp.repeat(request_rows[:, :, 1].reshape(-1), BLK)
    row_total = fetched.shape[0]
    wide = fetched.astype(jnp.float32)
    normed = wide * lax.rsqrt(jnp.mean(wide * wide, axis=1, keepdims=True) + 1e-06) * enc_gain
    enc_q = (
        jnp.dot(normed.astype(jnp.bfloat16), query_full, preferred_element_type=jnp.float32)
        * score_scale
    ).astype(jnp.bfloat16)
    scores = jnp.einsum(
        "nhd,khd->hnk",
        enc_q.reshape(row_total, enc_heads, HD),
        memory_keys,
        preferred_element_type=jnp.float32,
    )
    allowed = ((key_span[None, :] == span_rows[:, None]) & key_open[None, :])[None]
    scores = jnp.where(allowed, scores, masked_score)
    row_max = jnp.max(scores, axis=2, keepdims=True)
    weights_raw = jnp.where(allowed, jnp.exp(scores - row_max), 0.0)
    totals = jnp.sum(weights_raw, axis=2)
    context = jnp.einsum(
        "hnk,khd->nhd",
        weights_raw.astype(jnp.bfloat16),
        memory_values,
        preferred_element_type=jnp.float32,
    )
    context = (
        (context / totals.T[:, :, None]).astype(jnp.bfloat16).reshape(row_total, enc_heads * HD)
    )
    fetched = (wide + jnp.dot(context, output_full, preferred_element_type=jnp.float32)).astype(
        jnp.bfloat16
    )
    exchanged = lax.all_to_all(
        fetched.reshape(owners, slot_count, BLK, E), "nb", split_axis=0, concat_axis=0, tiled=True
    )
    weight_kv = cca_kv.reshape(E, 2 * head_cols)
    own_rows = exchanged.reshape(owners * capacity, BLK, E)[slot_index].reshape(
        request_count * BLK, E
    )
    group_kv = jnp.dot(
        lax.all_gather(own_rows, "nb", axis=0, tiled=True),
        weight_kv,
        preferred_element_type=jnp.float32,
    ).astype(jnp.bfloat16)
    span_count = span_offset.shape[0]
    group_kv = group_kv.reshape(span_count, K * R, 2 * head_cols)
    before = passed_along(group_kv[-1], "seq", 1)
    stacked = jnp.concatenate([before[None], group_kv], axis=0)
    cross_queries = q_cca.reshape(span_count, SPAN, head_count, HD)

    def attend_block(kv_set):
        key_rows = kv_set[:, :, :head_cols].reshape(span_count, K * R, head_count, HD)
        value_rows = kv_set[:, :, head_cols:].reshape(span_count, K * R, head_count, HD)
        scores = (
            jnp.einsum(
                "ichd,ikhd->ihck", cross_queries, key_rows, preferred_element_type=jnp.float32
            )
            * score_scale
        )
        row_max = jnp.max(scores, axis=3, keepdims=True)
        weights_raw = jnp.exp(scores - row_max)
        totals = jnp.sum(weights_raw, axis=3)
        summed = jnp.einsum(
            "ihck,ikhd->ichd",
            weights_raw.astype(jnp.bfloat16),
            value_rows,
            preferred_element_type=jnp.float32,
        )
        return summed / totals.transpose(0, 2, 1)[:, :, :, None]

    own_part = attend_block(stacked[1:])
    earlier = attend_block(stacked[:-1])
    see_own = (jnp.arange(SPAN, dtype=jnp.int32)[None, :] >= span_offset[:, None])[:, :, None, None]
    cca_out = jnp.where(see_own, own_part, earlier).reshape(tokens_here, head_cols)
    return (self_out + cca_out).astype(jnp.bfloat16)


def solution(mesh):
    in_specs = (
        P("seq", "nb"),
        P("seq", "nb"),
        P("seq", "nb"),
        P("seq", "nb"),
        P("seq", None, None),
        P(("seq", "nb"), None),
        P(("seq", "nb")),
        P("seq"),
        P("seq", None),
        P("seq", None),
        P(),
        P(None, None, "nb"),
    )
    out_specs = P("seq", "nb")
    return jax.shard_map(local, mesh=mesh, in_specs=in_specs, out_specs=out_specs, check_vma=False)
```

profile of v0, /device:TPU:1, one launch (start us, length us, event | category | flops | bytes accessed | tf_op | source)
XLA Modules:
  0.0 402.4 jit_solution(4048912258032524190)
XLA Ops:
  10.7 4.3 %all-to-all-start = ((s32[4,12,3]{1,2,0:T(4,128)}), s32[4,12,3]{1,2,0:T(4,128)S(1)}, u32[]{:S(2)}, u32[]{:S(2)}) async-start(s32[4,12,3]{1,2,0:T(4,128)} %copy.68), calls=%async_computation | async-start | bytes 16384 | tf_op jit(solution)/shard_map/all_to_all | solution.py:101
  19.5 3.5 copy.72
  29.7 4.4 %fusion.9 = bf16[768,2048]{1,0:T(8,128)(2,1)} fusion(bf16[48,16,2048]{2,1,0:T(8,128)(2,1)} %gather_fusion, f32[2048]{0:T(1024)S(1)} %copy-done.10, f32[768]{0:T(1024)S(1)} %rsqrt.12), kind=kLoop, calls=%fused_computation.15 | loop fusion | flops 6291456 | bytes 6302720 | tf_op jit(solution)/shard_map/convert_element_type | solution.py:109
  34.1 49.7 %all-gather.10.cloned.1.call-done = bf16[2048,1024]{1,0:T(8,128)(2,1)} async-done(((bf16[256,1024]{1,0:T(8,128)(2,1)}), bf16[2048,1024]{1,0:T(8,128)(2,1)}) %all-gather.10.cloned.1.call-update) | async-done | bytes 4194320 | tf_op jit(solution)/shard_map/all_gather | solution.py:71
  83.8 6.6 %fusion.30 = bf16[96,8,8,128]{3,2,1,0:T(8,128)(2,1)S(1)} fusion(bf16[768,2048]{1,0:T(8,128)(2,1)} %fusion.9, bf16[2048,1024]{1,0:T(8,128)(2,1)} %all-gather.10.cloned.1.call-done), kind=kOutput, calls=%fused_computation.44 | convolution fusion | flops 3222798336 | bytes 8912896 | tf_op jit(solution)/shard_map/dot_general | solution.py:109
  94.4 63.3 %all-gather.12.cloned.1.call-done = bf16[1024,2048]{1,0:T(8,128)(2,1)} async-done(((bf16[128,2048]{1,0:T(8,128)(2,1)}), bf16[1024,2048]{1,0:T(8,128)(2,1)}) %all-gather.12.cloned.1.call-update) | async-done | bytes 4194320 | tf_op jit(solution)/shard_map/all_gather | solution.py:72
  157.6 7.5 %fusion.10 = bf16[768,2048]{1,0:T(8,128)(2,1)} fusion(bf16[48,16,2048]{2,1,0:T(8,128)(2,1)} %gather_fusion, bf16[768,1024]{0,1:T(8,128)(2,1)S(1)} %bitcast.125, bf16[1024,2048]{1,0:T(8,128)(2,1)} %all-gather.12.cloned.1.call-done), kind=kOutput, calls=%fused_computation.16 | convolution fusion | flops 3225944064 | bytes 12058624 | tf_op jit(solution)/shard_map/dot_general | solution.py:132
  165.2 6.5 %all-to-all-start.1 = ((bf16[4,12,16,2048]{3,2,1,0:T(8,128)(2,1)}), bf16[4,12,16,2048]{3,2,1,0:T(8,128)(2,1)}, u32[]{:S(2)}, u32[]{:S(2)}) async-start(bf16[4,12,16,2048]{3,2,1,0:T(8,128)(2,1)} %bitcast.111), calls=%async_computation.1 | async-start | bytes 6291456 | tf_op jit(solution)/shard_map/all_to_all | solution.py:135
  171.7 36.2 %all-to-all-done.1 = bf16[4,12,16,2048]{3,2,1,0:T(8,128)(2,1)} async-done(((bf16[4,12,16,2048]{3,2,1,0:T(8,128)(2,1)}), bf16[4,12,16,2048]{3,2,1,0:T(8,128)(2,1)}, u32[]{:S(2)}, u32[]{:S(2)}) %all-to-all-start.1) | async-done | bytes 3145760 | tf_op jit(solution)/shard_map/all_to_all | solution.py:135
  207.8 3.5 gather_fusion.1
  211.4 10.2 %copy.96 = bf16[256,8,2,1024]{3,1,2,0:T(8,128)(2,1)} copy(bf16[256,8,2,1024]{3,2,1,0:T(2,128)(2,1)} %bitcast.114) | data formatting | bytes 16777216
  222.2 9.3 %all-gather.8.cloned.1.call-done = bf16[2048,1024]{1,0:T(8,128)(2,1)} async-done(((bf16[256,1024]{1,0:T(8,128)(2,1)}), bf16[2048,1024]{1,0:T(8,128)(2,1)}) %all-gather.8.cloned.1.call-update) | async-done | bytes 4194320 | tf_op jit(solution)/shard_map/all_gather | solution.py:45
  231.5 6.5 %copy.67 = bf16[2048,1024]{0,1:T(8,128)(2,1)} copy(bf16[2048,1024]{1,0:T(8,128)(2,1)} %all-gather.8.cloned.1.call-done) | data formatting | bytes 8388608 | tf_op jit(solution)/shard_map/all_gather | solution.py:45
  237.9 69.5 %all-gather.6.cloned.1.call-done = bf16[2048,1024]{0,1:T(8,128)(2,1)} async-done(((bf16[256,1024]{0,1:T(8,128)(2,1)}), bf16[2048,1024]{0,1:T(8,128)(2,1)}) %all-gather.6.cloned.1.call-update) | async-done | bytes 4194320 | tf_op jit(solution)/shard_map/all_gather | solution.py:44
  307.5 5.3 %fusion.1 = (f32[8,256]{1,0:T(8,128)S(1)}, f32[8,256,2048]{2,1,0:T(8,128)S(1)}) fusion(pred[256,2048]{1,0:T(8,128)(4,1)S(1)} %iota_compare_fusion, bf16[2048,8,128]{0,2,1:T(8,128)(2,1)} %bitcast.110, bf16[256,1024]{1,0:T(8,128)(2,1)S(1)} %copy-done.7), kind=kOutput, calls=%fused_computation.5 | convolution fusion | flops 1086322688 | bytes 22028288 | tf_op jit(solution)/shard_map/qhd,khd->hqk/dot_general | solution.py:48
  312.8 6.9 %copy-done.2 = f32[8,256,2048]{2,1,0:T(8,128)} copy-done((f32[8,256,2048]{2,1,0:T(8,128)}, f32[8,256,2048]{2,1,0:T(8,128)S(1)}, u32[]{:S(2)}) %copy-start.2) | copy-done | bytes 16777240
  319.7 5.0 %fusion.2 = f32[8,256]{1,0:T(8,128)S(1)} fusion(f32[8,256,2048]{2,1,0:T(8,128)S(1)} %get-tuple-element.23, f32[8,256]{1,0:T(8,128)S(1)} %broadcast_maximum_fusion, pred[256,2048]{1,0:T(8,128)(4,1)S(1)} %iota_compare_fusion), kind=kLoop, calls=%fused_computation.6 | loop fusion | flops 20969472 | bytes 17317888 | tf_op jit(solution)/shard_map/reduce_sum | solution.py:62
  324.7 17.7 %all-gather.14.cloned.1.call-done = bf16[1024,2048]{1,0:T(8,128)(2,1)} async-done(((bf16[256,2048]{1,0:T(8,128)(2,1)}), bf16[1024,2048]{1,0:T(8,128)(2,1)}) %all-gather.14.cloned.1.call-update) | async-done | bytes 4194320 | tf_op jit(solution)/shard_map/all_gather | solution.py:143
  342.4 12.6 %convolution_convert_fusion = bf16[1024,2048]{1,0:T(8,128)(2,1)S(1)} fusion(bf16[1024,2048]{1,0:T(8,128)(2,1)} %all-gather.14.cloned.1.call-done, bf16[2048,2048]{1,0:T(8,128)(2,1)} %bitcast.115), kind=kOutput, calls=%fused_computation.20 | convolution fusion | flops 8592031744 | bytes 16777216 | tf_op jit(solution)/shard_map/dot_general | solution.py:142
  358.0 4.1 %collective-permute-start = (bf16[256,2048]{1,0:T(8,128)(2,1)}, bf16[256,2048]{1,0:T(8,128)(2,1)}, u32[]{:S(2)}, u32[]{:S(2)}) collective-permute-start(bf16[256,2048]{1,0:T(8,128)(2,1)} %slice.48), channel_id=1, source_target_pairs={{0,4},{4,8},{8,12},{12,16},{16,20},{20,24},{24,28},{1,5},{5,9},{9,... | collective-permute-start | bytes 3145736 | tf_op jit(solution)/shard_map/ppermute | solution.py:20
  362.1 6.3 %fusion.44 = f32[256,8,128]{0,2,1:T(8,128)} fusion(bf16[2048,8,128]{0,2,1:T(8,128)(2,1)S(1)} %bitcast.120, f32[8,256,2048]{2,1,0:T(8,128)S(1)} %copy-done.3, f32[8,256]{1,0:T(8,128)S(1)} %broadcast_maximum_fusion, pred[256,2048]{1,0:T(8,128)(4,1)S(1)} %iota_compare_fusion, f32[256,8]{0,1:T(8,128)S(1)} %bitcast.131), kind=kOutput, calls=%fused_computation.57 | convolution fusion | flops 1094975488 | bytes 22560768 | tf_op jit(solution)/shard_map/hqk,khd->hqd/dot_general | solution.py:63
  370.0 6.2 %copy.74 = bf16[4,256,2048]{1,2,0:T(8,128)(2,1)} copy(bf16[4,256,2048]{2,1,0:T(8,128)(2,1)} %bitcast.116) | data formatting | bytes 8388608 | tf_op jit(solution)/shard_map/reshape | solution.py:148
  376.2 7.5 %collective-permute-done = bf16[256,2048]{1,0:T(8,128)(2,1)} collective-permute-done((bf16[256,2048]{1,0:T(8,128)(2,1)}, bf16[256,2048]{1,0:T(8,128)(2,1)}, u32[]{:S(2)}, u32[]{:S(2)}) %collective-permute-start) | collective-permute-done | bytes 1048608 | tf_op jit(solution)/shard_map/ppermute | solution.py:20
  385.1 3.8 pad_maximum_fusion
  (85 shorter events, 32.7 us)
Async XLA Ops:
  6.5 17.5 %copy-start = (bf16[256,2048]{1,0:T(8,128)(2,1)S(1)}, bf16[256,2048]{1,0:T(8,128)(2,1)}, u32[]{:S(2)}) copy-start(bf16[256,2048]{1,0:T(8,128)(2,1)} %param.17) | copy-start | bytes 3145732
  6.5 10.5 %copy-start.6 = (bf16[256,2,1024]{2,1,0:T(2,128)(2,1)S(1)}, bf16[256,2,1024]{2,1,0:T(2,128)(2,1)}, u32[]{:S(2)}) copy-start(bf16[256,2,1024]{2,1,0:T(2,128)(2,1)} %param.16) | copy-start | bytes 3145732
  6.5 77.3 %all-gather.10.cloned.1.call-start = ((), (), s32[]{:S(2)}) async-start(), calls=%async_computation.4 | async-start | bytes 4718592 | tf_op jit(solution)/shard_map/all_gather | solution.py:71
  7.3 150.4 %all-gather.12.cloned.1.call-start = ((), (), s32[]{:S(2)}) async-start(), calls=%async_computation.5 | async-start | bytes 4718592 | tf_op jit(solution)/shard_map/all_gather | solution.py:72
  8.0 11.3 %copy-start.11 = (s32[4]{0:T(128)S(1)}, s32[4]{0:T(128)}, u32[]{:S(2)}) copy-start(s32[4]{0:T(128)} %param.19) | copy-start | bytes 52
  8.0 223.5 %all-gather.8.cloned.1.call-start = ((), (), s32[]{:S(2)}) async-start(), calls=%async_computation.3 | async-start | bytes 4718592 | tf_op jit(solution)/shard_map/all_gather | solution.py:45
  10.7 13.2 %all-to-all-start = ((s32[4,12,3]{1,2,0:T(4,128)}), s32[4,12,3]{1,2,0:T(4,128)S(1)}, u32[]{:S(2)}, u32[]{:S(2)}) async-start(s32[4,12,3]{1,2,0:T(4,128)} %copy.68), calls=%async_computation | async-start | bytes 16384 | tf_op jit(solution)/shard_map/all_to_all | solution.py:101
  15.0 292.5 %all-gather.6.cloned.1.call-start = ((), (), s32[]{:S(2)}) async-start(), calls=%async_computation.2 | async-start | bytes 4718592 | tf_op jit(solution)/shard_map/all_gather | solution.py:44
  26.6 3.1 copy-start.10
  91.4 2.3 copy-start.8
  165.2 42.7 %all-to-all-start.1 = ((bf16[4,12,16,2048]{3,2,1,0:T(8,128)(2,1)}), bf16[4,12,16,2048]{3,2,1,0:T(8,128)(2,1)}, u32[]{:S(2)}, u32[]{:S(2)}) async-start(bf16[4,12,16,2048]{3,2,1,0:T(8,128)(2,1)} %bitcast.111), calls=%async_computation.1 | async-start | bytes 6291456 | tf_op jit(solution)/shard_map/all_to_all | solution.py:135
  171.7 170.7 %all-gather.14.cloned.1.call-start = ((), (), s32[]{:S(2)}) async-start(), calls=%async_computation.6 | async-start | bytes 5242880 | tf_op jit(solution)/shard_map/all_gather | solution.py:143
  211.4 10.2 %copy-start.9 = (bf16[256,1024]{1,0:T(8,128)(2,1)S(1)}, bf16[256,1024]{1,0:T(8,128)(2,1)}, u32[]{:S(2)}) copy-start(bf16[256,1024]{1,0:T(8,128)(2,1)} %param.15) | copy-start | bytes 1572868
  222.2 85.3 %copy-start.7 = (bf16[256,1024]{1,0:T(8,128)(2,1)S(1)}, bf16[256,1024]{1,0:T(8,128)(2,1)}, u32[]{:S(2)}) copy-start(bf16[256,1024]{1,0:T(8,128)(2,1)} %param.12) | copy-start | bytes 1572868
  312.7 7.0 %copy-start.2 = (f32[8,256,2048]{2,1,0:T(8,128)}, f32[8,256,2048]{2,1,0:T(8,128)S(1)}, u32[]{:S(2)}) copy-start(f32[8,256,2048]{2,1,0:T(8,128)S(1)} %get-tuple-element.23) | copy-start | bytes 50331652
  342.4 19.7 %copy-start.3 = (f32[8,256,2048]{2,1,0:T(8,128)S(1)}, f32[8,256,2048]{2,1,0:T(8,128)}, u32[]{:S(2)}) copy-start(f32[8,256,2048]{2,1,0:T(8,128)} %copy-done.2) | copy-start | bytes 50331652
  342.4 19.7 %copy-start.5 = (bf16[2048,1024]{0,1:T(8,128)(2,1)S(1)}, bf16[2048,1024]{0,1:T(8,128)(2,1)}, u32[]{:S(2)}) copy-start(bf16[2048,1024]{0,1:T(8,128)(2,1)} %copy.67) | copy-start | bytes 12582916
  355.0 1.9 copy-start.4
  358.0 25.7 %collective-permute-start = (bf16[256,2048]{1,0:T(8,128)(2,1)}, bf16[256,2048]{1,0:T(8,128)(2,1)}, u32[]{:S(2)}, u32[]{:S(2)}) collective-permute-start(bf16[256,2048]{1,0:T(8,128)(2,1)} %slice.48), channel_id=1, source_target_pairs={{0,4},{4,8},{8,12},{12,16},{16,20},{20,24},{24,28},{1,5},{5,9},{9,... | collective-permute-start | bytes 3145736 | tf_op jit(solution)/shard_map/ppermute | solution.py:20
  392.7 3.1 copy-start.1
Sparse Core Ops, SparseCore 0:
  9.5 74.2 all-gather.9
  85.9 71.6 all-gather.11
  159.8 71.6 all-gather.7
  233.4 74.0 all-gather.5
  308.9 33.4 all-gather.13
where the time goes:
time: 405 us; the launch traced here: 402 us
  waiting for transfers between devices  255 us (63%)
  local copies, waits for them, and re-layouts  52.7 us (13%)
  matrix products  43.6 us (11%)
  other arithmetic  22.4 us (6%)
  starting transfers between devices  15 us (4%)
  between operations  13.4 us (3%)
    all_gather x1, waiting for transfers between devices, local(): key_part = lax.all_gather(k_self, 'seq', axis=0, tiled=True)  69.5 us
    all_gather x1, waiting for transfers between devices, local(): lax.all_gather(enc_out, 'seq', axis=0, tiled=True)  63.3 us
    all_gather x1, waiting for transfers between devices, local(): lax.all_gather(enc_query, 'seq', axis=0, tiled=True)  49.7 us
    all_to_all x1, waiting for transfers between devices, local(): lax.all_to_all(fetched.reshape(owners, slot_count, BLK, E), 'nb', split_a...  36.2 us
    unnamed x28, local copies, waits for them, and re-layouts  22.2 us
    all_gather x1, waiting for transfers between devices, local(): lax.all_gather(own_rows, 'nb', axis=0, tiled=True)  17.7 us
    dot_general x1, matrix products, local(): jnp.dot(lax.all_gather(own_rows, 'nb', axis=0, tiled=True), weight_kv, pr...  12.6 us
    all_gather x1, waiting for transfers between devices, local(): value_part = lax.all_gather(v_self, 'seq', axis=0, tiled=True)  9.3 us
  transfers between devices with their start and end apart: 8, of which 7 were waited for; matrix products, arithmetic and copies ran while one was open for 21% of the time, Pallas kernels for 0%

commit v1 on v0

v1 whole, which is shorter than its diff:
```python
import functools

import jax
import jax.numpy as jnp
from jax import lax
from jax.experimental import pallas as pl
from jax.experimental.pallas import tpu as pltpu
from jax.sharding import PartitionSpec as P

HD = 128
SPAN = 64
K = 2
R = 128
BLK = 16
SET = K * R

masked_score = -1e30
MESH = pl.DeviceIdType.MESH
DOT_T = (((1,), (1,)), ((), ()))
LIMIT = 56 * 1024 * 1024


def greet(axis, count, me):
    barrier = pltpu.get_barrier_semaphore()
    for j in range(1, count):
        pl.semaphore_signal(
            barrier, inc=1, device_id={axis: lax.rem(me + j, count)}, device_id_type=MESH
        )
    pl.semaphore_wait(barrier, count - 1)


def causal_kernel(
    devices, per_peer, q_ref, k_ref, v_ref, out_ref, q_all, k_all, v_all, done,
    send_sem, recv_sem, own_sem, back_send, back_recv, back_own,
):
    me = lax.axis_index("seq")
    tokens = q_ref.shape[0]
    width = per_peer * HD
    greet("seq", devices, me)
    pairs = ((q_ref, q_all), (k_ref, k_all), (v_ref, v_all))

    def cols(index):
        return pl.ds(pl.multiple_of(index * width, HD), width)

    own = []
    for a, (src, dst) in enumerate(pairs):
        copy = pltpu.make_async_copy(src.at[:, cols(me)], dst.at[me], own_sem.at[a])
        copy.start()
        own.append(copy)
    sent = []
    for j in range(1, devices):
        peer = lax.rem(me + j, devices)
        for a, (src, dst) in enumerate(pairs):
            copy = pltpu.make_async_remote_copy(
                src_ref=src.at[:, cols(peer)],
                dst_ref=dst.at[me],
                send_sem=send_sem.at[a, j],
                recv_sem=recv_sem.at[a, me],
                device_id={"seq": peer},
                device_id_type=MESH,
            )
            copy.start()
            sent.append(copy)
    for copy in own:
        copy.wait()

    def arrived(dst, sem):
        pltpu.make_async_copy(dst, dst, sem).wait()

    row = lax.broadcasted_iota(jnp.int32, (tokens, tokens), 0)
    col = lax.broadcasted_iota(jnp.int32, (tokens, tokens), 1)
    open_here = col <= row
    for i in range(devices):
        @pl.when(me != i)
        def _(i=i):
            for a, (_, dst) in enumerate(pairs):
                arrived(dst.at[i], recv_sem.at[a, i])

        for h in range(per_peer):
            lanes = slice(h * HD, (h + 1) * HD)
            query = q_all[i, :, lanes]
            last = lax.dot_general(
                query, k_all[i, :, lanes], DOT_T, preferred_element_type=jnp.float32
            ) * (HD ** (-0.5))
            last = jnp.where(open_here, last, masked_score)
            top = jnp.max(last, axis=1, keepdims=True)
            if i:
                keys = k_all[0:i, :, lanes].reshape(i * tokens, HD)
                first = lax.dot_general(
                    query, keys, DOT_T, preferred_element_type=jnp.float32
                ) * (HD ** (-0.5))
                top = jnp.maximum(top, jnp.max(first, axis=1, keepdims=True))
            weights = jnp.where(open_here, jnp.exp(last - top), 0.0)
            total = jnp.sum(weights, axis=1, keepdims=True)
            summed = jnp.dot(
                weights.astype(jnp.bfloat16), v_all[i, :, lanes],
                preferred_element_type=jnp.float32,
            )
            if i:
                weights = jnp.exp(first - top)
                total += jnp.sum(weights, axis=1, keepdims=True)
                values = v_all[0:i, :, lanes].reshape(i * tokens, HD)
                summed += jnp.dot(
                    weights.astype(jnp.bfloat16), values, preferred_element_type=jnp.float32
                )
            done[i, :, lanes] = (summed / total).astype(done.dtype)

        @pl.when(me != i)
        def _(i=i):
            pltpu.make_async_remote_copy(
                src_ref=done.at[i],
                dst_ref=out_ref.at[:, cols(me)],
                send_sem=back_send.at[i],
                recv_sem=back_recv.at[me],
                device_id={"seq": i},
                device_id_type=MESH,
            ).start()

        @pl.when(me == i)
        def _(i=i):
            pltpu.make_async_copy(done.at[i], out_ref.at[:, cols(me)], back_own).start()

    for copy in sent:
        copy.wait_send()
    for i in range(devices):
        @pl.when(me != i)
        def _(i=i):
            arrived(done.at[i], back_send.at[i])
            arrived(out_ref.at[:, cols(i)], back_recv.at[i])

    arrived(out_ref.at[:, cols(me)], back_own)


def exchanged_attention(q, k, v, devices):
    tokens, head_cols = q.shape
    per_peer = head_cols // HD // devices
    width = per_peer * HD
    block = (devices, tokens, width)
    return pl.pallas_call(
        functools.partial(causal_kernel, devices, per_peer),
        name="self_attention",
        out_shape=jax.ShapeDtypeStruct((tokens, head_cols), jnp.bfloat16),
        in_specs=[pl.BlockSpec(memory_space=pl.ANY)] * 3,
        out_specs=pl.BlockSpec(memory_space=pltpu.VMEM),
        scratch_shapes=[pltpu.VMEM(block, jnp.bfloat16)] * 4
        + [
            pltpu.SemaphoreType.DMA((3, devices)),
            pltpu.SemaphoreType.DMA((3, devices)),
            pltpu.SemaphoreType.DMA((3,)),
            pltpu.SemaphoreType.DMA((devices,)),
            pltpu.SemaphoreType.DMA((devices,)),
            pltpu.SemaphoreType.DMA,
        ],
        compiler_params=pltpu.CompilerParams(
            collective_id=0, has_side_effects=True, vmem_limit_bytes=24 * 1024 * 1024
        ),
        cost_estimate=pl.CostEstimate(
            flops=2 * devices * devices * tokens * tokens * width,
            bytes_accessed=200 * 1000 * 1000,
            transcendentals=devices * devices * tokens * tokens * per_peer // 2,
        ),
    )(q, k, v)


def gathered_attention(q_self, k_self, v_self):
    tokens_here, head_cols = q_self.shape
    head_count = head_cols // HD
    query_pos = lax.axis_index("seq") * tokens_here + jnp.arange(tokens_here, dtype=jnp.int32)
    key_part = lax.all_gather(k_self, "seq", axis=0, tiled=True)
    value_part = lax.all_gather(v_self, "seq", axis=0, tiled=True)
    key_count = key_part.shape[0]
    scores = jnp.einsum(
        "qhd,khd->hqk",
        q_self.reshape(tokens_here, head_count, HD),
        key_part.reshape(key_count, head_count, HD),
        preferred_element_type=jnp.float32,
    ) * (HD ** (-0.5))
    key_pos = jnp.arange(key_count, dtype=jnp.int32)
    allowed = (key_pos[None, :] <= query_pos[:, None])[None]
    scores = jnp.where(allowed, scores, masked_score)
    top = jnp.max(scores, axis=2, keepdims=True)
    weights = jnp.where(allowed, jnp.exp(scores - top), 0.0)
    total = jnp.sum(weights, axis=2)
    added = jnp.einsum(
        "hqk,khd->hqd",
        weights.astype(jnp.bfloat16),
        value_part.reshape(key_count, head_count, HD),
        preferred_element_type=jnp.float32,
    )
    out = (added / total[:, :, None]).transpose(1, 0, 2).reshape(tokens_here, head_cols)
    return out.astype(jnp.bfloat16)


def encoder_kernel(
    spans, ids_ref, off_ref, db_ref, gain_ref, query_ref, key_ref, value_ref,
    ctx_ref, part_ref, nbr, sems,
):
    blocks = SET // BLK
    part = part_ref.shape[1]
    lane0 = pl.multiple_of(lax.axis_index("nb") * part, HD)

    def block_copy(i):
        rows = pl.ds(pl.multiple_of(i * BLK, BLK), BLK)
        source = pl.ds(pl.multiple_of(ids_ref[i] * BLK, BLK), BLK)
        return pltpu.make_async_copy(db_ref.at[source], nbr.at[rows], sems.at[i])

    @pl.loop(0, spans * blocks)
    def _(i):
        block_copy(i).start()

    gain = gain_ref[...]
    place = lax.broadcasted_iota(jnp.int32, (SET, SPAN), 1)
    for c in range(spans):
        @pl.loop(c * blocks, (c + 1) * blocks)
        def _(i):
            block_copy(i).wait()

        rows = slice(c * SET, (c + 1) * SET)
        wide = nbr[rows, :].astype(jnp.float32)
        mean = jnp.mean(wide * wide, axis=1, keepdims=True)
        normed = (wide * lax.rsqrt(mean + 1e-06) * gain).astype(jnp.bfloat16)
        eq = (
            jnp.dot(normed, query_ref[...], preferred_element_type=jnp.float32) * (HD ** (-0.5))
        ).astype(jnp.bfloat16)
        part_ref[rows, :] = nbr[rows, pl.ds(lane0, part)]
        keep = place < off_ref[c]
        for h in range(query_ref.shape[1] // HD):
            lanes = slice(h * HD, (h + 1) * HD)
            keys = key_ref[c * SPAN : (c + 1) * SPAN, lanes]
            values = value_ref[c * SPAN : (c + 1) * SPAN, lanes]
            scores = lax.dot_general(
                eq[:, lanes], keys, DOT_T, preferred_element_type=jnp.float32
            )
            scores = jnp.where(keep, scores, masked_score)
            top = jnp.max(scores, axis=1, keepdims=True)
            weights = jnp.where(keep, jnp.exp(scores - top), 0.0)
            total = jnp.sum(weights, axis=1, keepdims=True)
            summed = jnp.dot(
                weights.astype(jnp.bfloat16), values, preferred_element_type=jnp.float32
            )
            ctx_ref[rows, lanes] = (summed / total).astype(jnp.bfloat16)


def encoder_context(ids, offsets, db, gain, query, keys, values, part):
    spans = offsets.shape[0]
    rows = spans * SET
    width = db.shape[1]
    vmem = pl.BlockSpec(memory_space=pltpu.VMEM)
    smem = pl.BlockSpec(memory_space=pltpu.SMEM)
    return pl.pallas_call(
        functools.partial(encoder_kernel, spans),
        name="encoder_context",
        out_shape=(
            jax.ShapeDtypeStruct((rows, query.shape[1]), jnp.bfloat16),
            jax.ShapeDtypeStruct((rows, part), jnp.bfloat16),
        ),
        in_specs=[smem, smem, pl.BlockSpec(memory_space=pl.ANY), vmem, vmem, vmem, vmem],
        out_specs=(vmem, vmem),
        scratch_shapes=[
            pltpu.VMEM((rows, width), jnp.bfloat16),
            pltpu.SemaphoreType.DMA((spans * SET // BLK,)),
        ],
        compiler_params=pltpu.CompilerParams(vmem_limit_bytes=40 * 1024 * 1024),
        cost_estimate=pl.CostEstimate(
            flops=2 * rows * width * query.shape[1],
            bytes_accessed=30 * 1000 * 1000,
            transcendentals=0,
        ),
    )(ids, offsets, db, gain, query, keys, values)


def cross_kernel(
    devices, parts, spans, off_ref, enc_ref, weight_ref, q_ref, next_ref, self_ref, out_ref,
    kv, result, earlier, handed, landed, send_sem, recv_sem,
):
    me = lax.axis_index("seq")
    heads = q_ref.shape[1] // HD
    depth = enc_ref.shape[2]
    greet_next = lax.rem(me + 1, devices)
    barrier = pltpu.get_barrier_semaphore()
    for neighbour in (greet_next, lax.rem(me + devices - 1, devices)):
        pl.semaphore_signal(
            barrier, inc=1, device_id={"seq": neighbour}, device_id_type=MESH
        )
    pl.semaphore_wait(barrier, 2)
    copy = pltpu.make_async_remote_copy(
        src_ref=handed, dst_ref=landed, send_sem=send_sem, recv_sem=recv_sem,
        device_id={"seq": greet_next}, device_id_type=MESH,
    )
    for c in [spans - 1] + list(range(spans - 1)):
        rows = slice(c * SET, (c + 1) * SET)
        total = jnp.dot(
            enc_ref[0, rows, :], weight_ref[0:depth, :], preferred_element_type=jnp.float32
        )
        for n in range(1, parts):
            total += jnp.dot(
                enc_ref[n, rows, :], weight_ref[n * depth : (n + 1) * depth, :],
                preferred_element_type=jnp.float32,
            )
        kv[...] = total.astype(jnp.bfloat16)
        own_rows = slice(c * SPAN, (c + 1) * SPAN)
        for h in range(heads):
            lanes = slice(h * HD, (h + 1) * HD)
            if c == spans - 1:
                after = next_ref[:, lanes]
            else:
                after = q_ref[(c + 1) * SPAN : (c + 2) * SPAN, lanes]
            query = jnp.concatenate([q_ref[own_rows, lanes], after], axis=0)
            scores = lax.dot_general(
                query, kv[:, lanes], DOT_T, preferred_element_type=jnp.float32
            ) * (HD ** (-0.5))
            top = jnp.max(scores, axis=1, keepdims=True)
            weights = jnp.exp(scores - top)
            norm = jnp.sum(weights, axis=1, keepdims=True)
            summed = jnp.dot(
                weights.astype(jnp.bfloat16),
                kv[:, heads * HD + h * HD : heads * HD + (h + 1) * HD],
                preferred_element_type=jnp.float32,
            ) / norm
            result[own_rows, lanes] = summed[:SPAN]
            if c == spans - 1:
                handed[:, lanes] = summed[SPAN:]
            else:
                earlier[(c + 1) * SPAN : (c + 2) * SPAN, lanes] = summed[SPAN:]
        if c == spans - 1:
            copy.start()
    place = lax.broadcasted_iota(jnp.int32, (SPAN, q_ref.shape[1]), 0)
    for c in list(range(1, spans)) + [0]:
        rows = slice(c * SPAN, (c + 1) * SPAN)
        if c == 0:
            copy.wait()
            prior = jnp.where(me == 0, 0.0, landed[...])
        else:
            prior = earlier[rows, :]
        cross = jnp.where(place >= off_ref[c], result[rows, :], prior)
        out_ref[rows, :] = (self_ref[rows, :].astype(jnp.float32) + cross).astype(out_ref.dtype)


def cross_attention(offsets, enc, weight, q, after, self_out, devices):
    parts, rows, depth = enc.shape
    tokens, head_cols = q.shape
    spans = offsets.shape[0]
    vmem = pl.BlockSpec(memory_space=pltpu.VMEM)
    return pl.pallas_call(
        functools.partial(cross_kernel, devices, parts, spans),
        name="cross_attention",
        out_shape=jax.ShapeDtypeStruct((tokens, head_cols), jnp.bfloat16),
        in_specs=[pl.BlockSpec(memory_space=pltpu.SMEM)] + [vmem] * 5,
        out_specs=vmem,
        scratch_shapes=[
            pltpu.VMEM((SET, weight.shape[1]), jnp.bfloat16),
            pltpu.VMEM((tokens, head_cols), jnp.float32),
            pltpu.VMEM((tokens, head_cols), jnp.float32),
            pltpu.VMEM((SPAN, head_cols), jnp.float32),
            pltpu.VMEM((SPAN, head_cols), jnp.float32),
            pltpu.SemaphoreType.DMA,
            pltpu.SemaphoreType.DMA,
        ],
        compiler_params=pltpu.CompilerParams(
            collective_id=1, has_side_effects=True, vmem_limit_bytes=LIMIT
        ),
        cost_estimate=pl.CostEstimate(
            flops=2 * rows * parts * depth * weight.shape[1],
            bytes_accessed=20 * 1000 * 1000,
            transcendentals=0,
        ),
    )(offsets, enc, weight, q, after, self_out)


def own_share(array, axis):
    share = array.shape[axis] // lax.axis_size("nb")
    return lax.dynamic_slice_in_dim(array, lax.axis_index("nb") * share, share, axis)


def local(
    q_self, k_self, v_self, q_cca, memory, database, nbr_block, span_offset,
    enc_query, enc_out, enc_gain, cca_kv,
):
    devices = lax.axis_size("seq")
    owners = lax.axis_size("nb")
    head_cols = q_self.shape[1]
    ids = lax.all_gather(nbr_block, "nb", axis=0, tiled=True)
    db = lax.all_gather(database, "nb", axis=0, tiled=True)
    query_part = lax.all_gather(own_share(enc_query, 1), "seq", axis=0, tiled=True)
    output_part = lax.all_gather(own_share(enc_out, 1), "seq", axis=0, tiled=True)
    after = lax.ppermute(q_cca[:SPAN], "seq", [(i + 1, i) for i in range(devices - 1)])
    if (head_cols // HD) % devices == 0:
        self_out = exchanged_attention(q_self, k_self, v_self, devices)
    else:
        self_out = gathered_attention(q_self, k_self, v_self)
    ctx, nbr_part = encoder_context(
        ids, span_offset, db, enc_gain[None, :], query_part,
        own_share(memory[:, 0], 1), own_share(memory[:, 1], 1), output_part.shape[1],
    )
    ctx_full = lax.all_gather(ctx, "nb", axis=0)
    share = ctx.shape[1]
    update = sum(
        jnp.dot(
            ctx_full[n], output_part[n * share : (n + 1) * share],
            preferred_element_type=jnp.float32,
        )
        for n in range(owners)
    )
    encoded = (nbr_part.astype(jnp.float32) + update).astype(jnp.bfloat16)
    enc_full = lax.all_gather(encoded, "nb", axis=0)
    weight = cca_kv.reshape(cca_kv.shape[0], 2 * head_cols)
    return cross_attention(span_offset, enc_full, weight, q_cca, after, self_out, devices)


def solution(mesh):
    in_specs = (
        P("seq", "nb"),
        P("seq", "nb"),
        P("seq", "nb"),
        P("seq", "nb"),
        P("seq", None, None),
        P(("seq", "nb"), None),
        P(("seq", "nb")),
        P("seq"),
        P("seq", None),
        P("seq", None),
        P(),
        P(None, None, "nb"),
    )
    out_specs = P("seq", "nb")
    return jax.shard_map(local, mesh=mesh, in_specs=in_specs, out_specs=out_specs, check_vma=False)
```

time: 405 us -> 255 us (0.63)
  waiting for transfers between devices: 255 us -> 116 us
  Pallas kernels: 0 us -> 86.6 us
  matrix products: 43.6 us -> 5.22 us
  local copies, waits for them, and re-layouts: 52.7 us -> 24.3 us
  other arithmetic: 22.4 us -> 0 us
  starting transfers between devices: 15 us -> 1.64 us
  blocking collectives: 0 us -> 5.05 us
    all_gather x5, waiting for transfers between devices: 209 us -> 115 us  [the longest x1 36.2 us: local(): db = lax.all_gather(database, 'nb', axis=0, tiled=True)]
    pallas_call x0 -> x3, Pallas kernels: none -> 86.6 us  [the longest x1 47 us: exchanged_attention(): pl.pallas_call(functools.partial(causal_kernel, devices, per_peer), name=...]
    dot_general x11 -> x4, matrix products: 43.6 us -> 5.22 us  [local(): jnp.dot(ctx_full[n], output_part[n * share:(n + 1) * share], preferred_el...]
    all_to_all x2 -> x0, waiting for transfers between devices: 36.2 us -> none  [the longest x1 36.2 us: local(): lax.all_to_all(fetched.reshape(owners, slot_count, BLK, E), 'nb', split_a...]
    all_to_all x2 -> x0, starting transfers between devices: 10.8 us -> none  [the longest x1 6.51 us: local(): lax.all_to_all(fetched.reshape(owners, slot_count, BLK, E), 'nb', split_a...]
    reduce_sum x6 -> x0, other arithmetic: 9.39 us -> none  [the longest x1 5.01 us: local(): new_sum = jnp.sum(weights_raw, axis=2)]
    reshape x3 -> x0, local copies, waits for them, and re-layouts: 7.84 us -> none  [the longest x1 6.2 us: local(): group_kv = group_kv.reshape(span_count, K * R, 2 * head_cols)]
    ppermute x1, waiting for transfers between devices: 7.48 us -> 0.01 us  [local(): lax.ppermute(q_cca[:SPAN], 'seq', [(i + 1, i) for i in range(devices - 1)])]
  transfers between devices with their start and end apart: 8 -> 6, of which waited for: 7 -> 4; matrix products, arithmetic and copies ran while one was open for 21% -> 6% of each run, Pallas kernels for 0% -> 24%
where the time goes in v1:
time: 255 us; the launch traced here: 253 us
  waiting for transfers between devices  116 us (45%)
  Pallas kernels  86.6 us (34%)
  local copies, waits for them, and re-layouts  24.3 us (10%)
  between operations  14 us (5%)
  matrix products  5.22 us (2%)
  blocking collectives  5.05 us (2%)
    pallas_call x1, Pallas kernels, exchanged_attention(): pl.pallas_call(functools.partial(causal_kernel, devices, per_peer), name=...  47 us
    all_gather x1, waiting for transfers between devices, local(): db = lax.all_gather(database, 'nb', axis=0, tiled=True)  36.2 us
    all_gather x1, waiting for transfers between devices, local(): lax.all_gather(own_share(enc_query, 1), 'seq', axis=0, tiled=True)  31.3 us
    pallas_call x1, Pallas kernels, cross_attention(): pl.pallas_call(functools.partial(cross_kernel, devices, parts, spans), na...  25.4 us
    all_gather x1, waiting for transfers between devices, local(): ctx_full = lax.all_gather(ctx, 'nb', axis=0)  24.2 us
    all_gather x1, waiting for transfers between devices, local(): lax.all_gather(own_share(enc_out, 1), 'seq', axis=0, tiled=True)  23.2 us
    unnamed x37, local copies, waits for them, and re-layouts  19.1 us
    pallas_call x1, Pallas kernels, encoder_context(): pl.pallas_call(functools.partial(encoder_kernel, spans), name='encoder_co...  14.2 us
  transfers between devices with their start and end apart: 6, of which 4 were waited for; matrix products, arithmetic and copies ran while one was open for 6% of the time, Pallas kernels for 24%

profile of v1, /device:TPU:1, one launch (start us, length us, event | category | flops | bytes accessed | tf_op | source)
XLA Modules:
  0.0 252.5 jit_solution(11893949653482588298)
XLA Ops:
  6.5 1.0 copy-done
  7.6 0.7 constant_dynamic-slice_fusion.3
  8.3 0.7 all-gather.8.cloned.1.call-update
  9.1 1.6 constant_dynamic-slice_fusion
  10.8 1.5 fusion.11
  14.4 5.1 %all-reduce.ids_ref = s32[64]{0:T(128)S(1)} all-reduce(s32[64]{0:T(128)S(1)} %dynamic-update-slice), channel_id=1, replica_groups=mesh['seq'=8,'nb'=4] {'nb'}, use_global_device_ids=true, to_apply=%add | all-reduce | flops 64 | bytes 512
  19.5 31.3 %all-gather.10.cloned.1.call-done.query_ref = bf16[2048,256]{1,0:T(8,128)(2,1)} async-done(((bf16[256,256]{1,0:T(8,128)(2,1)}), bf16[2048,256]{1,0:T(8,128)(2,1)}) %all-gather.10.cloned.1.call-update) | async-done | bytes 1048592 | tf_op jit(solution)/shard_map/all_gather | solution.py:384
  50.8 36.2 %all-gather.8.cloned.1.call-done.db_ref = bf16[1024,2048]{1,0:T(8,128)(2,1)} async-done(((bf16[256,2048]{1,0:T(8,128)(2,1)}), bf16[1024,2048]{1,0:T(8,128)(2,1)}) %all-gather.8.cloned.1.call-update) | async-done | bytes 4194320 | tf_op jit(solution)/shard_map/all_gather | solution.py:383
  87.0 2.2 copy-done.1
  89.2 1.2 copy-done.2
  90.4 14.2 %encoder_context.1 = (bf16[1024,256]{1,0:T(8,128)(2,1)}, bf16[1024,512]{1,0:T(8,128)(2,1)S(1)}) custom-call(s32[64]{0:T(128)S(1)} %all-reduce.ids_ref, s32[4]{0:T(128)S(1)} %copy-done.4, bf16[1024,2048]{1,0:T(8,128)(2,1)S(1)} %copy-done.1, f32[1,2048]{1,0:T(1,128)S(1)} %bitcast.13, bf16[2048,256]{1,0:T(8,128)(2,1)S(1)} %copy-done.2, ...), custom_call_target="tpu_custom_call" | custom-call | flops 1073741824 | bytes 30000000 | tf_op jit(solution)/shard_map/encoder_context/pallas_call | solution.py:250
  104.7 23.2 %all-gather.12.cloned.1.call-done = bf16[1024,512]{1,0:T(8,128)(2,1)} async-done(((bf16[128,512]{1,0:T(8,128)(2,1)}), bf16[1024,512]{1,0:T(8,128)(2,1)}) %all-gather.12.cloned.1.call-update) | async-done | bytes 1048592 | tf_op jit(solution)/shard_map/all_gather | solution.py:385
  127.9 24.2 %all-gather.14.cloned.1.call-done = bf16[4096,256]{1,0:T(8,128)(2,1)} async-done(((bf16[1024,256]{1,0:T(8,128)(2,1)}), bf16[4096,256]{1,0:T(8,128)(2,1)}) %all-gather.14.cloned.1.call-update) | async-done | bytes 2097168 | tf_op jit(solution)/shard_map/all_gather | solution.py:395
  152.1 1.7 fusion.1
  153.9 1.5 fusion.3
  155.8 1.7 add_convert_fusion
  157.5 0.9 slice.43
  158.4 1.5 collective-permute-start
  159.9 10.3 %copy.19 = bf16[256,8,2,1024]{3,1,2,0:T(8,128)(2,1)} copy(bf16[256,8,2,1024]{3,2,1,0:T(2,128)(2,1)} %bitcast.14) | data formatting | bytes 16777216
  170.2 47.0 %self_attention.1.self_ref = bf16[256,1024]{1,0:T(8,128)(2,1)S(1)} custom-call(bf16[256,1024]{1,0:T(8,128)(2,1)S(1)} %copy-done.5, bf16[256,1024]{1,0:T(8,128)(2,1)S(1)} %copy-done.6, bf16[256,1024]{1,0:T(8,128)(2,1)S(1)} %copy-done.7), custom_call_target="tpu_custom_call" | custom-call | flops 1073741824 | bytes 200000000 | tf_op jit(solution)/shard_map/self_attention/pallas_call | solution.py:139
  217.2 0.8 copy-done.8
  218.0 0.6 copy-done.12
  218.7 25.4 %cross_attention.1 = bf16[256,1024]{1,0:T(8,128)(2,1)} custom-call(s32[4]{0:T(128)} %off_ref.3, bf16[4,1024,512]{2,1,0:T(8,128)(2,1)} %bitcast.16, bf16[2048,2048]{1,0:T(8,128)(2,1)} %bitcast.15, bf16[256,1024]{1,0:T(8,128)(2,1)} %q_ref.3, bf16[64,1024]{1,0:T(8,128)(2,1)} %copy-done.12, bf16[256,1024]{1,0:T(8,128)(2,1)} %copy-done.8), custom_call_target="tpu_custom_call" | custom-call | flops 8589934592 | bytes 20000000 | tf_op jit(solution)/shard_map/cross_attention/pallas_call | solution.py:344
  244.1 1.9 copy.26
  (43 shorter events, 2.3 us)
Async XLA Ops:
  6.5 1.0 copy-start
  6.5 4.2 %copy-start.9 = (bf16[256,2,1024]{2,1,0:T(2,128)(2,1)S(1)}, bf16[256,2,1024]{2,1,0:T(2,128)(2,1)}, u32[]{:S(2)}) copy-start(bf16[256,2,1024]{2,1,0:T(2,128)(2,1)} %param.16) | copy-start | bytes 3145732
  6.5 44.2 %all-gather.10.cloned.1.call-start = ((), (), s32[]{:S(2)}) async-start(), calls=%async_computation.1 | async-start | bytes 1179648 | tf_op jit(solution)/shard_map/all_gather | solution.py:384
  8.3 78.7 %all-gather.8.cloned.1.call-start = ((), (), s32[]{:S(2)}) async-start(), calls=%async_computation | async-start | bytes 5242880 | tf_op jit(solution)/shard_map/all_gather | solution.py:383
  9.0 118.9 %all-gather.12.cloned.1.call-start = ((), (), s32[]{:S(2)}) async-start(), calls=%async_computation.2 | async-start | bytes 1179648 | tf_op jit(solution)/shard_map/all_gather | solution.py:385
  10.7 141.4 %all-gather.14.cloned.1.call-start = ((), (), s32[]{:S(2)}) async-start(), calls=%async_computation.3 | async-start | bytes 2621440 | tf_op jit(solution)/shard_map/all_gather | solution.py:395
  10.7 2.2 copy-start.14
  10.7 3.4 %copy-start.13 = (s32[16]{0:T(128)S(1)}, s32[16]{0:T(128)}, u32[]{:S(2)}) copy-start(s32[16]{0:T(128)} %param.18) | copy-start | bytes 196
  10.8 76.2 %copy-start.3 = (f32[2048]{0:T(1024)S(1)}, f32[2048]{0:T(1024)}, u32[]{:S(2)}) copy-start(f32[2048]{0:T(1024)} %param.22) | copy-start | bytes 24580
  10.8 76.2 %copy-start.4 = (s32[4]{0:T(128)S(1)}, s32[4]{0:T(128)}, u32[]{:S(2)}) copy-start(s32[4]{0:T(128)} %off_ref.3) | copy-start | bytes 52
  87.0 2.2 copy-start.1
  89.2 1.2 copy-start.2
  104.6 113.4 %all-gather.16.cloned.1.call-start = ((), (), s32[]{:S(2)}) async-start(), calls=%async_computation.4 | async-start | bytes 5242880 | tf_op jit(solution)/shard_map/all_gather | solution.py:405
  152.1 1.8 copy-start.10
  153.9 1.5 copy-start.11
  158.4 59.6 %collective-permute-start = (bf16[64,1024]{1,0:T(8,128)(2,1)S(1)}, bf16[64,1024]{1,0:T(8,128)(2,1)S(1)}, u32[]{:S(2)}, u32[]{:S(2)}) collective-permute-start(bf16[64,1024]{1,0:T(8,128)(2,1)S(1)} %slice.43), channel_id=1, source_target_pairs={{4,0},{8,4},{12,8},{16,12},{20,16},{24,20},{28,24},{5,1},{9,5},{13... | collective-permute-start | bytes 393224 | tf_op jit(solution)/shard_map/ppermute | solution.py:386
  159.9 10.3 %copy-start.5 = (bf16[256,1024]{1,0:T(8,128)(2,1)S(1)}, bf16[256,1024]{1,0:T(8,128)(2,1)}, u32[]{:S(2)}) copy-start(bf16[256,1024]{1,0:T(8,128)(2,1)} %q_ref.2) | copy-start | bytes 1572868
  159.9 10.3 %copy-start.6 = (bf16[256,1024]{1,0:T(8,128)(2,1)S(1)}, bf16[256,1024]{1,0:T(8,128)(2,1)}, u32[]{:S(2)}) copy-start(bf16[256,1024]{1,0:T(8,128)(2,1)} %k_ref.1) | copy-start | bytes 1572868
  159.9 10.3 %copy-start.7 = (bf16[256,1024]{1,0:T(8,128)(2,1)S(1)}, bf16[256,1024]{1,0:T(8,128)(2,1)}, u32[]{:S(2)}) copy-start(bf16[256,1024]{1,0:T(8,128)(2,1)} %v_ref.1) | copy-start | bytes 1572868
  217.2 0.8 copy-start.8
  218.0 0.6 copy-start.12
Sparse Core Ops, SparseCore 0:
  9.5 41.2 all-gather.9
  52.3 34.6 all-gather.7
  89.1 38.7 all-gather.11
  129.3 22.7 all-gather.13
  157.6 34.5 all-gather.15

commit v2 on v1

--- a/solution.py
+++ b/solution.py
@@ -20,23 +20,76 @@
 LIMIT = 56 * 1024 * 1024
 
 
-def greet(axis, count, me):
+CORES = 2
+
+
+class Group:
+    def __init__(self, count):
+        self.count = count
+        self.me = lax.axis_index("nb")
+        self.partner = self.me + 1 - 2 * lax.rem(self.me, CORES)
+        self.chips = count // CORES
+
+    def far(self, j, of=None):
+        return lax.rem((self.me if of is None else of) + CORES * j, self.count)
+
+    def targets(self):
+        return [self.partner] + [self.far(j) for j in range(1, self.chips)]
+
+    def share(self, slot_ref, source, send_sem, recv_sem):
+        copies = []
+        for t, peer in enumerate(self.targets()):
+            copy = pltpu.make_async_remote_copy(
+                src_ref=source, dst_ref=slot_ref(self.me), send_sem=send_sem(t),
+                recv_sem=recv_sem(self.me), device_id={"nb": peer}, device_id_type=MESH,
+            )
+            copy.start()
+            copies.append(copy)
+        return copies
+
+    def pass_on(self, slot_ref, send_sem, recv_sem):
+        copies = []
+        for j in range(1, self.chips):
+            slot = self.far(j)
+            arrived(slot_ref(slot), recv_sem(slot))
+            copy = pltpu.make_async_remote_copy(
+                src_ref=slot_ref(slot), dst_ref=slot_ref(slot),
+                send_sem=send_sem(self.chips + j - 1), recv_sem=recv_sem(slot),
+                device_id={"nb": self.partner}, device_id_type=MESH,
+            )
+            copy.start()
+            copies.append(copy)
+        return copies
+
+    def finish(self, slot_ref, recv_sem):
+        for j in range(self.chips):
+            slot = self.far(j, self.partner)
+            arrived(slot_ref(slot), recv_sem(slot))
+
+
+def arrived(dst, sem):
+    pltpu.make_async_copy(dst, dst, sem).wait()
+
+
+def greet(targets):
     barrier = pltpu.get_barrier_semaphore()
-    for j in range(1, count):
-        pl.semaphore_signal(
-            barrier, inc=1, device_id={axis: lax.rem(me + j, count)}, device_id_type=MESH
-        )
-    pl.semaphore_wait(barrier, count - 1)
+    for target in targets:
+        pl.semaphore_signal(barrier, inc=1, device_id=target, device_id_type=MESH)
+    pl.semaphore_wait(barrier, len(targets))
 
 
 def causal_kernel(
-    devices, per_peer, q_ref, k_ref, v_ref, out_ref, q_all, k_all, v_all, done,
-    send_sem, recv_sem, own_sem, back_send, back_recv, back_own,
+    devices, owners, per_peer, q_ref, k_ref, v_ref, db_ref, out_ref, db_out, q_all, k_all, v_all,
+    done, send_sem, recv_sem, own_sem, back_send, back_recv, back_own, db_send, db_recv, db_own,
 ):
     me = lax.axis_index("seq")
     tokens = q_ref.shape[0]
     width = per_peer * HD
-    greet("seq", devices, me)
+    group = Group(owners)
+    greet(
+        [{"seq": lax.rem(me + j, devices)} for j in range(1, devices)]
+        + [{"nb": peer} for peer in group.targets()]
+    )
     pairs = ((q_ref, q_all), (k_ref, k_all), (v_ref, v_all))
 
     def cols(index):
@@ -61,11 +114,13 @@
             )
             copy.start()
             sent.append(copy)
+    db_slot = lambda slot: db_out.at[slot]
+    db_sems = (lambda t: db_send.at[t], lambda slot: db_recv.at[slot])
+    db_copies = group.share(db_slot, db_ref, *db_sems)
+    own_db = pltpu.make_async_copy(db_ref, db_slot(group.me), db_own)
+    own_db.start()
     for copy in own:
         copy.wait()
-
-    def arrived(dst, sem):
-        pltpu.make_async_copy(dst, dst, sem).wait()
 
     row = lax.broadcasted_iota(jnp.int32, (tokens, tokens), 0)
     col = lax.broadcasted_iota(jnp.int32, (tokens, tokens), 1)
@@ -120,7 +175,12 @@
         def _(i=i):
             pltpu.make_async_copy(done.at[i], out_ref.at[:, cols(me)], back_own).start()
 
-    for copy in sent:
+        if i == devices // 2:
+            db_copies += group.pass_on(db_slot, *db_sems)
+
+    own_db.wait()
+    group.finish(db_slot, db_sems[1])
+    for copy in sent + db_copies:
         copy.wait_send()
     for i in range(devices):
         @pl.when(me != i)
@@ -131,17 +191,20 @@
     arrived(out_ref.at[:, cols(me)], back_own)
 
 
-def exchanged_attention(q, k, v, devices):
+def exchanged_attention(q, k, v, db, devices, owners):
     tokens, head_cols = q.shape
     per_peer = head_cols // HD // devices
     width = per_peer * HD
     block = (devices, tokens, width)
     return pl.pallas_call(
-        functools.partial(causal_kernel, devices, per_peer),
+        functools.partial(causal_kernel, devices, owners, per_peer),
         name="self_attention",
-        out_shape=jax.ShapeDtypeStruct((tokens, head_cols), jnp.bfloat16),
-        in_specs=[pl.BlockSpec(memory_space=pl.ANY)] * 3,
-        out_specs=pl.BlockSpec(memory_space=pltpu.VMEM),
+        out_shape=(
+            jax.ShapeDtypeStruct((tokens, head_cols), jnp.bfloat16),
+            jax.ShapeDtypeStruct((owners,) + db.shape, db.dtype),
+        ),
+        in_specs=[pl.BlockSpec(memory_space=pl.ANY)] * 4,
+        out_specs=(pl.BlockSpec(memory_space=pltpu.VMEM), pl.BlockSpec(memory_space=pl.ANY)),
         scratch_shapes=[pltpu.VMEM(block, jnp.bfloat16)] * 4
         + [
             pltpu.SemaphoreType.DMA((3, devices)),
@@ -150,6 +213,9 @@
             pltpu.SemaphoreType.DMA((devices,)),
             pltpu.SemaphoreType.DMA((devices,)),
             pltpu.SemaphoreType.DMA,
+            pltpu.SemaphoreType.DMA((owners,)),
+            pltpu.SemaphoreType.DMA((owners,)),
+            pltpu.SemaphoreType.DMA,
         ],
         compiler_params=pltpu.CompilerParams(
             collective_id=0, has_side_effects=True, vmem_limit_bytes=24 * 1024 * 1024
@@ -159,7 +225,7 @@
             bytes_accessed=200 * 1000 * 1000,
             transcendentals=devices * devices * tokens * tokens * per_peer // 2,
         ),
-    )(q, k, v)
+    )(q, k, v, db)
 
 
 def gathered_attention(q_self, k_self, v_self):
@@ -270,25 +336,54 @@
 
 
 def cross_kernel(
-    devices, parts, spans, off_ref, enc_ref, weight_ref, q_ref, next_ref, self_ref, out_ref,
-    kv, result, earlier, handed, landed, send_sem, recv_sem,
+    devices, parts, spans, off_ref, ctx_ref, outw_ref, nbr_ref, weight_ref, q_ref, next_ref,
+    self_ref, out_ref, enc_ref, kv, result, earlier, handed, landed, send_sem, recv_sem,
+    enc_send, enc_recv,
 ):
     me = lax.axis_index("seq")
     heads = q_ref.shape[1] // HD
     depth = enc_ref.shape[2]
+    share = ctx_ref.shape[2]
     greet_next = lax.rem(me + 1, devices)
-    barrier = pltpu.get_barrier_semaphore()
-    for neighbour in (greet_next, lax.rem(me + devices - 1, devices)):
-        pl.semaphore_signal(
-            barrier, inc=1, device_id={"seq": neighbour}, device_id_type=MESH
+    group = Group(parts)
+    greet(
+        [{"seq": greet_next}, {"seq": lax.rem(me + devices - 1, devices)}]
+        + [{"nb": peer} for peer in group.targets()]
+    )
+    order = [spans - 1] + list(range(spans - 1))
+    enc_copies = []
+
+    def wiring(c):
+        rows = pl.ds(c * SET, SET)
+        return (
+            lambda slot: enc_ref.at[slot, rows],
+            lambda t: enc_send.at[t, c],
+            lambda slot: enc_recv.at[slot, c],
         )
-    pl.semaphore_wait(barrier, 2)
+
+    for c in order:
+        rows = slice(c * SET, (c + 1) * SET)
+        total = nbr_ref[rows, :].astype(jnp.float32)
+        update = jnp.dot(
+            ctx_ref[0, rows, :], outw_ref[0:share, :], preferred_element_type=jnp.float32
+        )
+        for n in range(1, parts):
+            update += jnp.dot(
+                ctx_ref[n, rows, :], outw_ref[n * share : (n + 1) * share, :],
+                preferred_element_type=jnp.float32,
+            )
+        enc_ref[group.me, rows, :] = (total + update).astype(jnp.bfloat16)
+        slot_ref, sends, recvs = wiring(c)
+        enc_copies += group.share(slot_ref, slot_ref(group.me), sends, recvs)
     copy = pltpu.make_async_remote_copy(
         src_ref=handed, dst_ref=landed, send_sem=send_sem, recv_sem=recv_sem,
         device_id={"seq": greet_next}, device_id_type=MESH,
     )
-    for c in [spans - 1] + list(range(spans - 1)):
+    for c in order:
         rows = slice(c * SET, (c + 1) * SET)
+        slot_ref, sends, recvs = wiring(c)
+        enc_copies += group.pass_on(slot_ref, sends, recvs)
+        group.finish(slot_ref, recvs)
         total = jnp.dot(
             enc_ref[0, rows, :], weight_ref[0:depth, :], preferred_element_type=jnp.float32
         )
@@ -334,10 +429,13 @@
             prior = earlier[rows, :]
         cross = jnp.where(place >= off_ref[c], result[rows, :], prior)
         out_ref[rows, :] = (self_ref[rows, :].astype(jnp.float32) + cross).astype(out_ref.dtype)
-
-
-def cross_attention(offsets, enc, weight, q, after, self_out, devices):
-    parts, rows, depth = enc.shape
+    for copy in enc_copies:
+        copy.wait_send()
+
+
+def cross_attention(offsets, ctx, output_part, nbr_part, weight, q, after, self_out, devices):
+    parts = ctx.shape[0]
+    rows, depth = nbr_part.shape
     tokens, head_cols = q.shape
     spans = offsets.shape[0]
     vmem = pl.BlockSpec(memory_space=pltpu.VMEM)
@@ -345,9 +443,10 @@
         functools.partial(cross_kernel, devices, parts, spans),
         name="cross_attention",
         out_shape=jax.ShapeDtypeStruct((tokens, head_cols), jnp.bfloat16),
-        in_specs=[pl.BlockSpec(memory_space=pltpu.SMEM)] + [vmem] * 5,
+        in_specs=[pl.BlockSpec(memory_space=pltpu.SMEM)] + [vmem] * 7,
         out_specs=vmem,
         scratch_shapes=[
+            pltpu.VMEM((parts, rows, depth), jnp.bfloat16),
             pltpu.VMEM((SET, weight.shape[1]), jnp.bfloat16),
             pltpu.VMEM((tokens, head_cols), jnp.float32),
             pltpu.VMEM((tokens, head_cols), jnp.float32),
@@ -355,6 +454,8 @@
             pltpu.VMEM((SPAN, head_cols), jnp.float32),
             pltpu.SemaphoreType.DMA,
             pltpu.SemaphoreType.DMA,
+            pltpu.SemaphoreType.DMA((parts, spans)),
+            pltpu.SemaphoreType.DMA((parts, spans)),
         ],
         compiler_params=pltpu.CompilerParams(
             collective_id=1, has_side_effects=True, vmem_limit_bytes=LIMIT
@@ -364,7 +465,7 @@
             bytes_accessed=20 * 1000 * 1000,
             transcendentals=0,
         ),
-    )(offsets, enc, weight, q, after, self_out)
+    )(offsets, ctx, output_part, nbr_part, weight, q, after, self_out)
 
 
 def own_share(array, axis):
@@ -380,31 +481,24 @@
     owners = lax.axis_size("nb")
     head_cols = q_self.shape[1]
     ids = lax.all_gather(nbr_block, "nb", axis=0, tiled=True)
-    db = lax.all_gather(database, "nb", axis=0, tiled=True)
     query_part = lax.all_gather(own_share(enc_query, 1), "seq", axis=0, tiled=True)
     output_part = lax.all_gather(own_share(enc_out, 1), "seq", axis=0, tiled=True)
     after = lax.ppermute(q_cca[:SPAN], "seq", [(i + 1, i) for i in range(devices - 1)])
     if (head_cols // HD) % devices == 0:
-        self_out = exchanged_attention(q_self, k_self, v_self, devices)
+        self_out, db = exchanged_attention(q_self, k_self, v_self, database, devices, owners)
+        db = db.reshape(-1, database.shape[1])
     else:
+        db = lax.all_gather(database, "nb", axis=0, tiled=True)
         self_out = gathered_attention(q_self, k_self, v_self)
     ctx, nbr_part = encoder_context(
         ids, span_offset, db, enc_gain[None, :], query_part,
         own_share(memory[:, 0], 1), own_share(memory[:, 1], 1), output_part.shape[1],
     )
     ctx_full = lax.all_gather(ctx, "nb", axis=0)
-    share = ctx.shape[1]
-    update = sum(
-        jnp.dot(
-            ctx_full[n], output_part[n * share : (n + 1) * share],
-            preferred_element_type=jnp.float32,
-        )
-        for n in range(owners)
-    )
-    encoded = (nbr_part.astype(jnp.float32) + update).astype(jnp.bfloat16)
-    enc_full = lax.all_gather(encoded, "nb", axis=0)
     weight = cca_kv.reshape(cca_kv.shape[0], 2 * head_cols)
-    return cross_attention(span_offset, enc_full, weight, q_cca, after, self_out, devices)
+    return cross_attention(
+        span_offset, ctx_full, output_part, nbr_part, weight, q_cca, after, self_out, devices
+    )
 
 
 def solution(mesh):

time: 255 us -> 189 us (0.74)
  waiting for transfers between devices: 116 us -> 26.7 us
  Pallas kernels: 86.6 us -> 107 us
  local copies, waits for them, and re-layouts: 24.3 us -> 34 us
  matrix products: 5.22 us -> 0 us
    all_gather x2 -> x0, waiting for transfers between devices: 36.2 us -> none  [the longest x1 36.2 us: local(): db = lax.all_gather(database, 'nb', axis=0, tiled=True)]
    all_gather x1, waiting for transfers between devices: 31.3 us -> 0.01 us  [local(): lax.all_gather(own_share(enc_query, 1), 'seq', axis=0, tiled=True)]
    all_gather x1, waiting for transfers between devices: 23.2 us -> 2.14 us  [local(): lax.all_gather(own_share(enc_out, 1), 'seq', axis=0, tiled=True)]
    pallas_call x1, Pallas kernels: 25.4 us -> 38.7 us  [cross_attention(): pl.pallas_call(functools.partial(cross_kernel, devices, parts, spans), na...]
    unnamed x37 -> x33, local copies, waits for them, and re-layouts: 19.1 us -> 26.8 us
    pallas_call x1, Pallas kernels: 47 us -> 54.6 us  [exchanged_attention(): pl.pallas_call(functools.partial(causal_kernel, devices, owners, per_peer...]
    dot_general x4 -> x0, matrix products: 5.22 us -> none  [local(): jnp.dot(ctx_full[n], output_part[n * share:(n + 1) * share], preferred_el...]
  transfers between devices with their start and end apart: 6 -> 4, of which waited for: 4 -> 2; matrix products, arithmetic and copies ran while one was open for 6% -> 10% of each run, Pallas kernels for 24% -> 37%
where the time goes in v2:
time: 189 us
  Pallas kernels  107 us (57%)
  local copies, waits for them, and re-layouts  34 us (18%)
  waiting for transfers between devices  26.7 us (14%)
  between operations  13.9 us (7%)
  blocking collectives  5.05 us (3%)
    pallas_call x1, Pallas kernels, exchanged_attention(): pl.pallas_call(functools.partial(causal_kernel, devices, owners, per_peer...  54.6 us
    pallas_call x1, Pallas kernels, cross_attention(): pl.pallas_call(functools.partial(cross_kernel, devices, parts, spans), na...  38.7 us
    unnamed x33, local copies, waits for them, and re-layouts  26.8 us
    all_gather x1, waiting for transfers between devices, local(): ctx_full = lax.all_gather(ctx, 'nb', axis=0)  24.6 us
    pallas_call x1, Pallas kernels, encoder_context(): pl.pallas_call(functools.partial(encoder_kernel, spans), name='encoder_co...  14.2 us
    unnamed x1, blocking collectives  5.05 us
  transfers between devices with their start and end apart: 4, of which 2 were waited for; matrix products, arithmetic and copies ran while one was open for 10% of the time, Pallas kernels for 37%

profile of v2, /device:TPU:1, one launch (start us, length us, event | category | flops | bytes accessed | tf_op | source)
XLA Modules:
  0.0 188.5 jit_solution(5783495859597826459)
XLA Ops:
  6.6 1.0 copy-done
  8.3 1.6 constant_dynamic-slice_fusion
  10.0 3.4 %fusion = (bf16[256,1,1024]{2,1,0:T(2,128)(2,1)S(1)}, bf16[256,1,1024]{2,1,0:T(2,128)(2,1)S(1)}) fusion(bf16[256,2,1024]{2,1,0:T(2,128)(2,1)} %param.16), kind=kLoop, calls=%fused_computation.6 | loop fusion | bytes 2097152 | tf_op jit(solution)/shard_map/slice | solution.py:495
  14.0 1.3 dynamic-slice.2
  15.9 0.9 dynamic-update-slice
  16.7 5.1 %all-reduce.ids_ref = s32[64]{0:T(128)S(1)} all-reduce(s32[64]{0:T(128)S(1)} %dynamic-update-slice), channel_id=1, replica_groups=mesh['seq'=8,'nb'=4] {'nb'}, use_global_device_ids=true, to_apply=%add | all-reduce | flops 64 | bytes 512
  21.8 1.2 copy-done.6
  23.0 1.0 copy-done.8
  24.1 1.0 copy-done.9
  25.1 1.0 copy-done.10
  26.1 54.6 %self_attention.1 = (bf16[256,1024]{1,0:T(8,128)(2,1)S(1)}, bf16[4,256,2048]{2,1,0:T(8,128)(2,1)S(1)}) custom-call(bf16[256,1024]{1,0:T(8,128)(2,1)S(1)} %copy-done.8, bf16[256,1024]{1,0:T(8,128)(2,1)S(1)} %copy-done.9, bf16[256,1024]{1,0:T(8,128)(2,1)S(1)} %copy-done.10, bf16[256,2048]{1,0:T(8,128)(2,1)S(1)} %copy-done.6), custom_call_target="tpu_custom_call" | custom-call | flops 1073741824 | bytes 200000000 | tf_op jit(solution)/shard_map/self_attention/pallas_call | solution.py:199
  80.7 1.9 %copy-done.1 = bf16[4,256,2048]{2,1,0:T(8,128)(2,1)} copy-done((bf16[4,256,2048]{2,1,0:T(8,128)(2,1)}, bf16[4,256,2048]{2,1,0:T(8,128)(2,1)S(1)}, u32[]{:S(2)}) %copy-start.1) | copy-done | bytes 4194328
  82.7 0.8 copy-done.11
  83.5 2.2 %copy-done.2 = bf16[4,256,2048]{2,1,0:T(8,128)(2,1)S(1)} copy-done((bf16[4,256,2048]{2,1,0:T(8,128)(2,1)S(1)}, bf16[4,256,2048]{2,1,0:T(8,128)(2,1)}, u32[]{:S(2)}) %copy-start.2) | copy-done | bytes 4194328
  85.8 1.2 copy-done.3
  87.0 14.2 %encoder_context.1 = (bf16[1024,256]{1,0:T(8,128)(2,1)}, bf16[1024,512]{1,0:T(8,128)(2,1)S(1)}) custom-call(s32[64]{0:T(128)S(1)} %all-reduce.ids_ref, s32[4]{0:T(128)S(1)} %copy-done.5, bf16[1024,2048]{1,0:T(8,128)(2,1)S(1)} %bitcast.12, f32[1,2048]{1,0:T(1,128)S(1)} %bitcast.15, bf16[2048,256]{1,0:T(8,128)(2,1)S(1)} %copy-done.3, ...), custom_call_target="tpu_custom_call" | custom-call | flops 1073741824 | bytes 30000000 | tf_op jit(solution)/shard_map/encoder_context/pallas_call | solution.py:316
  101.2 1.0 copy-done.7
  102.3 1.0 slice.11
  103.2 1.3 collective-permute-start
  104.5 10.2 %copy.19 = bf16[256,8,2,1024]{3,1,2,0:T(8,128)(2,1)} copy(bf16[256,8,2,1024]{3,2,1,0:T(2,128)(2,1)} %bitcast.16) | data formatting | bytes 16777216
  114.7 2.1 %all-gather.7.cloned.1.call-done.outw_ref = bf16[1024,512]{1,0:T(8,128)(2,1)} async-done(((bf16[128,512]{1,0:T(8,128)(2,1)}), bf16[1024,512]{1,0:T(8,128)(2,1)}) %all-gather.7.cloned.1.call-update) | async-done | bytes 1048592 | tf_op jit(solution)/shard_map/all_gather | solution.py:485
  116.9 24.6 %all-gather.9.cloned.1.call-done = bf16[4096,256]{1,0:T(8,128)(2,1)} async-done(((bf16[1024,256]{1,0:T(8,128)(2,1)}), bf16[4096,256]{1,0:T(8,128)(2,1)}) %all-gather.9.cloned.1.call-update) | async-done | bytes 2097168 | tf_op jit(solution)/shard_map/all_gather | solution.py:497
  141.4 38.7 %cross_attention.1 = bf16[256,1024]{1,0:T(8,128)(2,1)} custom-call(s32[4]{0:T(128)} %off_ref.3, bf16[4,1024,256]{2,1,0:T(8,128)(2,1)} %bitcast.18, bf16[1024,512]{1,0:T(8,128)(2,1)} %all-gather.7.cloned.1.call-done.outw_ref, bf16[1024,512]{1,0:T(8,128)(2,1)} %copy-done.7, bf16[2048,2048]{1,0:T(8,128)(2,1)} %bitcast.17, bf16[256,1024]{1,0:T(8,128)(2,1)} %q_ref.3, ...), custom_call_target="tpu_custom_call" | custom-call | flops 8589934592 | bytes 20000000 | tf_op jit(solution)/shard_map/cross_attention/pallas_call | solution.py:442
  180.1 1.9 copy.26
  (29 shorter events, 1.4 us)
Async XLA Ops:
  6.5 1.0 copy-start
  6.5 77.0 %copy-start.5 = (s32[4]{0:T(128)S(1)}, s32[4]{0:T(128)}, u32[]{:S(2)}) copy-start(s32[4]{0:T(128)} %off_ref.3) | copy-start | bytes 52
  6.5 77.0 %copy-start.4 = (f32[2048]{0:T(1024)S(1)}, f32[2048]{0:T(1024)}, u32[]{:S(2)}) copy-start(f32[2048]{0:T(1024)} %param.22) | copy-start | bytes 24580
  6.5 77.0 %all-gather.5.cloned.1.call-start = ((), (), s32[]{:S(2)}) async-start(), calls=%async_computation | async-start | bytes 1179648 | tf_op jit(solution)/shard_map/all_gather | solution.py:484
  8.3 108.6 %all-gather.7.cloned.1.call-start = ((), (), s32[]{:S(2)}) async-start(), calls=%async_computation.1 | async-start | bytes 1179648 | tf_op jit(solution)/shard_map/all_gather | solution.py:485
  9.9 131.5 %all-gather.9.cloned.1.call-start = ((), (), s32[]{:S(2)}) async-start(), calls=%async_computation.2 | async-start | bytes 2621440 | tf_op jit(solution)/shard_map/all_gather | solution.py:497
  21.8 1.2 copy-start.6
  23.0 1.0 copy-start.8
  24.1 1.0 copy-start.9
  25.1 1.0 copy-start.10
  80.7 1.9 %copy-start.1 = (bf16[4,256,2048]{2,1,0:T(8,128)(2,1)}, bf16[4,256,2048]{2,1,0:T(8,128)(2,1)S(1)}, u32[]{:S(2)}) copy-start(bf16[4,256,2048]{2,1,0:T(8,128)(2,1)S(1)} %get-tuple-element.9) | copy-start | bytes 12582916
  82.7 0.8 copy-start.11
  83.5 2.2 %copy-start.2 = (bf16[4,256,2048]{2,1,0:T(8,128)(2,1)S(1)}, bf16[4,256,2048]{2,1,0:T(8,128)(2,1)}, u32[]{:S(2)}) copy-start(bf16[4,256,2048]{2,1,0:T(8,128)(2,1)} %copy-done.1) | copy-start | bytes 12582916
  85.8 1.2 copy-start.3
  101.2 1.0 copy-start.7
  103.2 11.5 %collective-permute-start = (bf16[64,1024]{1,0:T(8,128)(2,1)S(1)}, bf16[64,1024]{1,0:T(8,128)(2,1)S(1)}, u32[]{:S(2)}, u32[]{:S(2)}) collective-permute-start(bf16[64,1024]{1,0:T(8,128)(2,1)S(1)} %slice.11), channel_id=1, source_target_pairs={{4,0},{8,4},{12,8},{16,12},{20,16},{24,20},{28,24},{5,1},{9,5},{13... | collective-permute-start | bytes 393224 | tf_op jit(solution)/shard_map/ppermute | solution.py:486
  114.7 26.7 %copy-start.12 = (bf16[64,1024]{1,0:T(8,128)(2,1)}, bf16[64,1024]{1,0:T(8,128)(2,1)S(1)}, u32[]{:S(2)}) copy-start(bf16[64,1024]{1,0:T(8,128)(2,1)S(1)} %collective-permute-done.next_ref) | copy-start | bytes 393220
Sparse Core Ops, SparseCore 0:
  9.5 60.7 all-gather.4
  72.4 44.4 all-gather.6
  118.4 22.9 all-gather.8

commit v3 on v2

--- a/solution.py
+++ b/solution.py
@@ -218,7 +218,7 @@
             pltpu.SemaphoreType.DMA,
         ],
         compiler_params=pltpu.CompilerParams(
-            collective_id=0, has_side_effects=True, vmem_limit_bytes=24 * 1024 * 1024
+            collective_id=0, has_side_effects=True, vmem_limit_bytes=LIMIT
         ),
         cost_estimate=pl.CostEstimate(
             flops=2 * devices * devices * tokens * tokens * width,
@@ -326,13 +326,61 @@
             pltpu.VMEM((rows, width), jnp.bfloat16),
             pltpu.SemaphoreType.DMA((spans * SET // BLK,)),
         ],
-        compiler_params=pltpu.CompilerParams(vmem_limit_bytes=40 * 1024 * 1024),
+        compiler_params=pltpu.CompilerParams(vmem_limit_bytes=LIMIT),
         cost_estimate=pl.CostEstimate(
             flops=2 * rows * width * query.shape[1],
             bytes_accessed=30 * 1000 * 1000,
             transcendentals=0,
         ),
     )(ids, offsets, db, gain, query, keys, values)
+
+
+def gather_kernel(owners, chunks, src_ref, out_ref, send_sem, recv_sem, own_sem):
+    group = Group(owners)
+    greet([{"nb": peer} for peer in group.targets()])
+    own = pltpu.make_async_copy(src_ref, out_ref.at[group.me], own_sem)
+    own.start()
+    size = src_ref.shape[0] // chunks
+
+    def wiring(c):
+        rows = pl.ds(c * size, size)
+        return (
+            lambda slot: out_ref.at[slot, rows],
+            lambda t: send_sem.at[t, c],
+            lambda slot: recv_sem.at[slot, c],
+        )
+
+    copies = []
+    for c in range(chunks):
+        slot_ref, sends, recvs = wiring(c)
+        copies += group.share(slot_ref, src_ref.at[pl.ds(c * size, size)], sends, recvs)
+    for c in range(chunks):
+        copies += group.pass_on(*wiring(c))
+    for c in range(chunks):
+        slot_ref, _, recvs = wiring(c)
+        group.finish(slot_ref, recvs)
+    own.wait()
+    for copy in copies:
+        copy.wait_send()
+
+
+def gathered(block, owners, chunks):
+    vmem = pl.BlockSpec(memory_space=pltpu.VMEM)
+    return pl.pallas_call(
+        functools.partial(gather_kernel, owners, chunks),
+        name="context_gather",
+        out_shape=jax.ShapeDtypeStruct((owners,) + block.shape, block.dtype),
+        in_specs=[vmem],
+        out_specs=vmem,
+        scratch_shapes=[
+            pltpu.SemaphoreType.DMA((owners, chunks)),
+            pltpu.SemaphoreType.DMA((owners, chunks)),
+            pltpu.SemaphoreType.DMA,
+        ],
+        compiler_params=pltpu.CompilerParams(
+            collective_id=2, has_side_effects=True, vmem_limit_bytes=24 * 1024 * 1024
+        ),
+    )(block)
 
 
 def cross_kernel(
@@ -494,7 +542,7 @@
         ids, span_offset, db, enc_gain[None, :], query_part,
         own_share(memory[:, 0], 1), own_share(memory[:, 1], 1), output_part.shape[1],
     )
-    ctx_full = lax.all_gather(ctx, "nb", axis=0)
+    ctx_full = gathered(ctx, owners, span_offset.shape[0])
     weight = cca_kv.reshape(cca_kv.shape[0], 2 * head_cols)
     return cross_attention(
         span_offset, ctx_full, output_part, nbr_part, weight, q_cca, after, self_out, devices

time: 189 us -> 178 us (0.942)
  waiting for transfers between devices: 26.7 us -> 0.04 us
  Pallas kernels: 107 us -> 131 us
  local copies, waits for them, and re-layouts: 34 us -> 25.5 us
    all_gather x1 -> x0, waiting for transfers between devices: 24.6 us -> none  [local(): ctx_full = lax.all_gather(ctx, 'nb', axis=0)]
    pallas_call x0 -> x1, Pallas kernels: none -> 15.8 us  [gathered(): pl.pallas_call(functools.partial(gather_kernel, owners, chunks), name='co...]
    unnamed x33 -> x19, local copies, waits for them, and re-layouts: 26.8 us -> 18.4 us
    pallas_call x1, Pallas kernels: 54.6 us -> 62 us  [exchanged_attention(): pl.pallas_call(functools.partial(causal_kernel, devices, owners, per_peer...]
    pallas_call x1, Pallas kernels: 38.7 us -> 43.2 us  [cross_attention(): pl.pallas_call(functools.partial(cross_kernel, devices, parts, spans), na...]
    pallas_call x1, Pallas kernels: 14.2 us -> 10.4 us  [encoder_context(): pl.pallas_call(functools.partial(encoder_kernel, spans), name='encoder_co...]
    all_gather x1, waiting for transfers between devices: 2.14 us -> 0.01 us  [local(): lax.all_gather(own_share(enc_out, 1), 'seq', axis=0, tiled=True)]
  transfers between devices with their start and end apart: 4 -> 3, of which waited for: 2 -> 0; matrix products, arithmetic and copies ran while one was open for 10% -> 11% of each run, Pallas kernels for 37% -> 50%
where the time goes in v3:
time: 178 us
  Pallas kernels  131 us (74%)
  local copies, waits for them, and re-layouts  25.5 us (14%)
  between operations  14.2 us (8%)
  blocking collectives  5.57 us (3%)
    pallas_call x1, Pallas kernels, exchanged_attention(): pl.pallas_call(functools.partial(causal_kernel, devices, owners, per_peer...  62 us
    pallas_call x1, Pallas kernels, cross_attention(): pl.pallas_call(functools.partial(cross_kernel, devices, parts, spans), na...  43.2 us
    unnamed x19, local copies, waits for them, and re-layouts  18.4 us
    pallas_call x1, Pallas kernels, gathered(): pl.pallas_call(functools.partial(gather_kernel, owners, chunks), name='co...  15.8 us
    pallas_call x1, Pallas kernels, encoder_context(): pl.pallas_call(functools.partial(encoder_kernel, spans), name='encoder_co...  10.4 us
    unnamed x1, blocking collectives  5.57 us
  transfers between devices with their start and end apart: 3, of which 0 were waited for; matrix products, arithmetic and copies ran while one was open for 11% of the time, Pallas kernels for 50%

profile of v3, /device:TPU:1, one launch (start us, length us, event | category | flops | bytes accessed | tf_op | source)
XLA Modules:
  0.0 178.0 jit_solution(16640943383194696523)
XLA Ops:
  6.5 1.0 copy-done
  7.6 0.7 constant_dynamic-slice_fusion.3
  8.2 0.0 all-gather.3.cloned.1.call-update
  8.3 0.0 all-gather.5.cloned.1.call-start
  8.3 1.6 constant_dynamic-slice_fusion
  9.9 0.0 all-gather.5.cloned.1.call-update
  9.9 0.9 slice.11
  10.8 1.3 collective-permute-start
  12.1 3.4 %fusion = (bf16[256,1,1024]{2,1,0:T(2,128)(2,1)S(1)}, bf16[256,1,1024]{2,1,0:T(2,128)(2,1)S(1)}) fusion(bf16[256,2,1024]{2,1,0:T(2,128)(2,1)} %param.16), kind=kLoop, calls=%fused_computation.6 | loop fusion | bytes 2097152 | tf_op jit(solution)/shard_map/slice | solution.py:543
  15.5 0.5 constant_dynamic-slice_fusion.1
  16.1 62.0 %self_attention.1 = (bf16[256,1024]{1,0:T(8,128)(2,1)}, bf16[4,256,2048]{2,1,0:T(8,128)(2,1)}) custom-call(bf16[256,1024]{1,0:T(8,128)(2,1)} %q_ref.2, bf16[256,1024]{1,0:T(8,128)(2,1)} %k_ref.1, bf16[256,1024]{1,0:T(8,128)(2,1)} %v_ref.1, bf16[256,2048]{1,0:T(8,128)(2,1)} %db_ref.1), custom_call_target="tpu_custom_call" | custom-call | flops 1073741824 | bytes 200000000 | tf_op jit(solution)/shard_map/self_attention/pallas_call | solution.py:199
  78.1 0.7 copy.22
  78.8 0.7 copy.23
  79.5 10.2 %copy.19 = bf16[256,8,2,1024]{3,1,2,0:T(8,128)(2,1)} copy(bf16[256,8,2,1024]{3,2,1,0:T(2,128)(2,1)} %bitcast.11) | data formatting | bytes 16777216
  89.6 0.7 dynamic-slice.2
  91.0 0.2 dynamic-update-slice
  91.2 5.6 %all-reduce.ids_ref = s32[64]{0:T(128)} all-reduce(s32[64]{0:T(128)S(1)} %dynamic-update-slice), channel_id=1, replica_groups=mesh['seq'=8,'nb'=4] {'nb'}, use_global_device_ids=true, to_apply=%add | all-reduce | flops 64 | bytes 512
  96.8 10.4 %encoder_context.1 = (bf16[1024,256]{1,0:T(8,128)(2,1)}, bf16[1024,512]{1,0:T(8,128)(2,1)}) custom-call(s32[64]{0:T(128)} %all-reduce.ids_ref, s32[4]{0:T(128)} %off_ref.3, bf16[1024,2048]{1,0:T(8,128)(2,1)} %bitcast.13, f32[1,2048]{1,0:T(1,128)} %bitcast.16, bf16[2048,256]{1,0:T(8,128)(2,1)} %all-gather.3.cloned.1.call-done.query_ref, ...), custom_call_target="tpu_custom_call" | custom-call | flops 1073741824 | bytes 30000000 | tf_op jit(solution)/shard_map/encoder_context/pallas_call | solution.py:316
  107.2 1.0 copy-done.2
  108.2 15.8 %context_gather.1.ctx_ref = bf16[4,1024,256]{2,1,0:T(8,128)(2,1)S(1)} custom-call(bf16[1024,256]{1,0:T(8,128)(2,1)S(1)} %copy-done.2), custom_call_target="tpu_custom_call" | custom-call | tf_op jit(solution)/shard_map/context_gather/pallas_call | solution.py:369
  124.0 1.4 copy-done.1
  125.4 0.7 copy-done.3
  126.1 43.2 %cross_attention.1 = bf16[256,1024]{1,0:T(8,128)(2,1)} custom-call(s32[4]{0:T(128)} %off_ref.3, bf16[4,1024,256]{2,1,0:T(8,128)(2,1)} %copy-done.1, bf16[1024,512]{1,0:T(8,128)(2,1)} %all-gather.5.cloned.1.call-done.outw_ref, bf16[1024,512]{1,0:T(8,128)(2,1)} %get-tuple-element.11.nbr_ref, bf16[2048,2048]{1,0:T(8,128)(2,1)} %bitcast.12, ...), custom_call_target="tpu_custom_call" | custom-call | flops 8589934592 | bytes 20000000 | tf_op jit(solution)/shard_map/cross_attention/pallas_call | solution.py:490
  169.3 1.9 %copy.26 = bf16[256,1024]{1,0:T(8,128)(2,1)} copy(bf16[256,1024]{1,0:T(8,128)(2,1)} %cross_attention.1) | data formatting | bytes 1048576
  (13 shorter events, 0.0 us)
Async XLA Ops:
  6.5 1.0 copy-start
  6.5 90.3 %all-gather.3.cloned.1.call-start = ((), (), s32[]{:S(2)}) async-start(), calls=%async_computation | async-start | bytes 1179648 | tf_op jit(solution)/shard_map/all_gather | solution.py:532
  8.3 117.1 %all-gather.5.cloned.1.call-start = ((), (), s32[]{:S(2)}) async-start(), calls=%async_computation.1 | async-start | bytes 1179648 | tf_op jit(solution)/shard_map/all_gather | solution.py:533
  10.8 114.6 %collective-permute-start = (bf16[64,1024]{1,0:T(8,128)(2,1)S(1)}, bf16[64,1024]{1,0:T(8,128)(2,1)S(1)}, u32[]{:S(2)}, u32[]{:S(2)}) collective-permute-start(bf16[64,1024]{1,0:T(8,128)(2,1)S(1)} %slice.11), channel_id=1, source_target_pairs={{4,0},{8,4},{12,8},{16,12},{20,16},{24,20},{28,24},{5,1},{9,5},{13... | collective-permute-start | bytes 393224 | tf_op jit(solution)/shard_map/ppermute | solution.py:534
  79.4 10.2 %copy-start.5 = (u32[32]{0:T(128)S(1)}, u32[32]{0:T(128)}, u32[]{:S(2)}) copy-start(u32[32]{0:T(128)} %constant.20) | copy-start | bytes 388
  79.4 11.5 %copy-start.4 = (s32[16]{0:T(128)S(1)}, s32[16]{0:T(128)}, u32[]{:S(2)}) copy-start(s32[16]{0:T(128)} %param.18) | copy-start | bytes 196
  107.2 1.0 copy-start.2
  124.0 1.4 copy-start.1
  125.4 0.7 copy-start.3
Sparse Core Ops, SparseCore 0:
  9.5 62.1 all-gather.2
  73.8 42.5 all-gather.4
